TPU v7x, 32 devices: a whole 2x2x4 slice. The times are simulated.
32 devices in a mesh: branch: 2 (over x), sky: 16 (over z, y, core).
Axes of the slice: x: 2, y: 2, z: 4, core: 2. Of those that a mesh axis runs over, the one named last changes fastest.
Arguments:
- sky_maps: bfloat16 [2, 64, 4096], P('branch', None, 'sky'), may hold values from -6 to 6
- footprint: int32 [2, 4096], P('branch', 'sky'), may hold values 0 or 1
- neighbours: int32 [9, 4096], P(None, 'sky'), may hold values from -1 to 4095, as said below
- enc_weight: bfloat16 [2, 6, 9, 64, 64], P('branch'), may hold values from -0.1875 to 0.1875
- join_weight: bfloat16 [256, 128], P(None, 'branch'), may hold values from -0.5 to 0.5
- dec_weight: bfloat16 [9, 256, 256], P(None, 'branch'), may hold values from -0.125 to 0.125
- cotangent: bfloat16 [256, 4096], P('branch', 'sky'), may hold values from -6 to 6
Outputs:
- map_grads: bfloat16 [2, 64, 4096], P('branch', None, 'sky')
- weight_grads: float32 [2, 6, 9, 64, 64], P('branch')
Inputs may be any that keep to these rules, and one draw needn't show every extreme that they name: `neighbours`: slot 4 of each row is the row itself; every other entry is -1 or a row index that differs from the row's own by at most 256.
All inputs are finite; a program needn't handle non-finite values. No bound on the sum of `footprint` on one device may be relied on, other than what follows from the above.
Results may differ from a plain program's by a relative error of at most 0.017.
Values may be sent and summed in bfloat16 or wider, within the bound.
A program may use at most 64 MiB of HBM per device.

v0:
```python
import functools
import math

import jax
import jax.numpy as jnp
from jax import lax
from jax.experimental import pallas as pl
from jax.experimental.pallas import tpu as pltpu
from jax.sharding import PartitionSpec as P

MESH = pl.DeviceIdType.MESH
F32 = jnp.float32
BF16 = jnp.bfloat16


def matmul(a, b, contract=((1,), (0,))):
    return lax.dot_general(a, b, (contract, ((), ())), preferred_element_type=F32)


def kernel(
    n_sky, n_branch,
    maps, foot, nb, enc, join, dec, cot,
    map_out, grad_out,
    own, from_left, from_right, picked, slope, one_hot, one_hot_t, rel, enc_flat, enc_t,
    grad, edge_left, edge_right, back_left, back_right,
    dec_acc, rim_left, rim_right, got_left, got_right, unit_own, unit_send, unit_got,
    join_got, top_got,
    fwd_send, fwd_recv, bwd_send, bwd_recv, rim_send, rim_recv, br_send, br_recv,
):
    depth, taps = enc.shape[0], enc.shape[1]
    chans, rows = maps.shape
    sky = lax.axis_index("sky")
    branch = lax.axis_index("branch")
    has_left, has_right = sky > 0, sky < n_sky - 1
    left, right = jnp.maximum(sky - 1, 0), jnp.minimum(sky + 1, n_sky - 1)
    peers = [(d, lax.rem(branch + d, n_branch)) for d in range(1, n_branch)]

    barrier = pltpu.get_barrier_semaphore()

    @pl.when(has_left)
    def _():
        pl.semaphore_signal(barrier, inc=1, device_id={"sky": left}, device_id_type=MESH)

    @pl.when(has_right)
    def _():
        pl.semaphore_signal(barrier, inc=1, device_id={"sky": right}, device_id_type=MESH)

    for _, peer in peers:
        pl.semaphore_signal(barrier, inc=1, device_id={"branch": peer}, device_id_type=MESH)
    pl.semaphore_wait(
        barrier, has_left.astype(jnp.int32) + has_right.astype(jnp.int32) + (n_branch - 1)
    )

    def to_left(src, dst, send, recv):
        return pltpu.make_async_remote_copy(
            src_ref=src, dst_ref=dst, send_sem=send, recv_sem=recv,
            device_id={"sky": left}, device_id_type=MESH,
        )

    def to_right(src, dst, send, recv):
        return pltpu.make_async_remote_copy(
            src_ref=src, dst_ref=dst, send_sem=send, recv_sem=recv,
            device_id={"sky": right}, device_id_type=MESH,
        )

    def halo(layer):
        return (
            to_left(own.at[layer], from_right.at[layer], fwd_send.at[layer, 0], fwd_recv.at[layer, 0]),
            to_right(own.at[layer], from_left.at[layer], fwd_send.at[layer, 1], fwd_recv.at[layer, 1]),
        )

    def back(layer):
        return (
            to_left(edge_left.at[layer], back_right.at[layer], bwd_send.at[layer, 0], bwd_recv.at[layer, 0]),
            to_right(edge_right.at[layer], back_left.at[layer], bwd_send.at[layer, 1], bwd_recv.at[layer, 1]),
        )

    def rims():
        return (
            to_left(rim_left, got_right, rim_send.at[0], rim_recv.at[0]),
            to_right(rim_right, got_left, rim_send.at[1], rim_recv.at[1]),
        )

    def start(pair):
        @pl.when(has_left)
        def _():
            pair[0].start()

        @pl.when(has_right)
        def _():
            pair[1].start()

    def wait_recv(pair):
        @pl.when(has_right)
        def _():
            pair[0].wait_recv()

        @pl.when(has_left)
        def _():
            pair[1].wait_recv()

    def wait_send(pair):
        @pl.when(has_left)
        def _():
            pair[0].wait_send()

        @pl.when(has_right)
        def _():
            pair[1].wait_send()

    def across(src, dst, kind):
        return [
            pltpu.make_async_remote_copy(
                src_ref=src, dst_ref=dst.at[d - 1],
                send_sem=br_send.at[kind, d - 1], recv_sem=br_recv.at[kind, d - 1],
                device_id={"branch": peer}, device_id_type=MESH,
            )
            for d, peer in peers
        ]

    own[0] = maps[...]
    start(halo(0))
    join_copies = across(join, join_got, 0)
    for copy in join_copies:
        copy.start()

    @pl.when(jnp.logical_not(has_left))
    def _():
        from_left[...] = jnp.zeros_like(from_left)
        back_left[...] = jnp.zeros_like(back_left)
        got_left[...] = jnp.zeros_like(got_left)

    @pl.when(jnp.logical_not(has_right))
    def _():
        from_right[...] = jnp.zeros_like(from_right)
        back_right[...] = jnp.zeros_like(back_right)
        got_right[...] = jnp.zeros_like(got_right)

    first = (sky - 1) * rows
    near = nb[...]
    offset = jnp.where(near >= 0, near - first, -1)
    part = jnp.where(
        offset < 0, -1,
        jnp.where(offset < rows, offset + rows, jnp.where(offset < 2 * rows, offset - rows, offset)),
    )
    rel[...] = jnp.full(rel.shape, -1, jnp.int32)
    rel[0:taps, :] = part
    col = jnp.transpose(rel[...])
    for k in range(taps):
        lanes = slice(k * rows, (k + 1) * rows)
        line = rel[k : k + 1, :]
        for p in range(3):
            index = lax.broadcasted_iota(jnp.int32, (rows, rows), 0) + p * rows
            one_hot[p * rows : (p + 1) * rows, lanes] = jnp.where(line == index, 1.0, 0.0).astype(BF16)
            index = lax.broadcasted_iota(jnp.int32, (rows, rows), 1) + p * rows
            one_hot_t[lanes, p * rows : (p + 1) * rows] = jnp.where(
                col[:, k : k + 1] == index, 1.0, 0.0
            ).astype(BF16)

    retained = foot[...].astype(F32)
    dec_acc[...] = jnp.zeros_like(dec_acc)
    dec_steps = 3

    @pl.loop(0, depth)
    def forward(layer):
        hidden = own[layer]
        for k in range(taps):
            block = matmul(hidden, one_hot[0:rows, k * rows : (k + 1) * rows])
            picked[layer, k * chans : (k + 1) * chans, :] = block.astype(BF16)
        for k in range(taps):
            tap = enc[layer, k]
            enc_flat[layer, :, k * chans : (k + 1) * chans] = tap
            enc_t[layer, k * chans : (k + 1) * chans, :] = jnp.transpose(tap)

        @pl.when(layer < dec_steps)
        def _():
            each = taps // dec_steps
            parts = []
            for j in range(each):
                term = matmul(dec[layer * each + j], cot[...], ((0,), (0,)))
                parts.append(term.astype(BF16))
            span = each * rows
            table = one_hot_t[pl.ds(pl.multiple_of(layer * span, span), span), :]
            dec_acc[...] += matmul(jnp.concatenate(parts, axis=1), table)

        @pl.when(layer == dec_steps)
        def _():
            rim_left[...] = dec_acc[:, rows : 2 * rows].astype(BF16)
            rim_right[...] = dec_acc[:, 2 * rows : 3 * rows].astype(BF16)
            start(rims())

        @pl.when(layer == dec_steps + 1)
        def _():
            wait_recv(rims())
            total = dec_acc[:, 0:rows] + got_left[...].astype(F32) + got_right[...].astype(F32)
            unit_own[...] = total
            unit_send[...] = total.astype(BF16)
            for copy in across(unit_send, unit_got, 1):
                copy.start()

        wait_recv(halo(layer))
        for k in range(taps):
            lanes = slice(k * rows, (k + 1) * rows)
            both = jnp.concatenate([from_left[layer], from_right[layer]], axis=1)
            block = matmul(both, one_hot[rows : 3 * rows, lanes])
            at = slice(k * chans, (k + 1) * chans)
            picked[layer, at, :] = picked[layer, at, :] + block.astype(BF16)
        pre = matmul(enc_flat[layer], picked[layer])
        sig = jax.nn.sigmoid(pre)
        after = retained * (hidden.astype(F32) + pre * sig)
        own[layer + 1] = after.astype(BF16)

        @pl.when(layer < depth - 1)
        def _():
            start(halo(layer + 1))

        slope[layer] = sig * (1.0 + pre * (1.0 - sig))

    top_copies = across(own.at[depth], top_got, 2)
    for copy in top_copies:
        copy.start()
    joined = matmul(join[...], own[depth])
    for copy in join_copies:
        copy.wait_recv()
    unit_copies = across(unit_send, unit_got, 1)
    unit = unit_own[...]
    for i, copy in enumerate(unit_copies):
        copy.wait_recv()
        unit = unit + unit_got[i].astype(F32)
    for i, copy in enumerate(top_copies):
        copy.wait_recv()
        joined = joined + matmul(join_got[i], top_got[i])
    sig = jax.nn.sigmoid(joined)
    unit_slope = (sig * (1.0 + joined * (1.0 - sig))).astype(BF16).astype(F32)
    unit_grad = (unit * unit_slope).astype(BF16)
    grad[...] = matmul(join[...], unit_grad, ((0,), (0,)))

    @pl.loop(0, depth)
    def backward(step):
        layer = depth - 1 - step
        masked = retained * grad[...]
        act = (masked * slope[layer]).astype(BF16)
        terms = matmul(enc_t[layer], act).astype(BF16)
        terms = jnp.concatenate(
            [terms[k * chans : (k + 1) * chans] for k in range(taps)], axis=1
        )
        edge = matmul(terms, one_hot_t[:, rows : 3 * rows]).astype(BF16)
        edge_left[layer] = edge[:, :rows]
        edge_right[layer] = edge[:, rows:]
        start(back(layer))
        inner = masked + matmul(terms, one_hot_t[:, 0:rows])
        weight = matmul(act, picked[layer], ((1,), (1,)))
        for k in range(taps):
            grad_out[layer, k] = weight[:, k * chans : (k + 1) * chans]
        wait_recv(back(layer))
        grad[...] = inner + back_left[layer].astype(F32) + back_right[layer].astype(F32)

    map_out[...] = grad[...].astype(BF16)

    @pl.loop(0, depth)
    def drain(layer):
        wait_send(halo(layer))
        wait_send(back(layer))

    wait_send(rims())
    for copy in join_copies + unit_copies + top_copies:
        copy.wait_send()


def per_device(n_sky, n_branch, sky_maps, footprint, neighbours, enc_weight, join_weight, dec_weight, cotangent):
    chans, rows = sky_maps.shape[1:]
    depth, taps = enc_weight.shape[1:3]
    width = dec_weight.shape[2]
    others = max(n_branch - 1, 1)
    vmem = pltpu.VMEM
    dma = pltpu.SemaphoreType.DMA
    layers = (depth, chans, rows)
    scratch = [
        vmem((depth + 1, chans, rows), BF16),
        vmem(layers, BF16),
        vmem(layers, BF16),
        vmem((depth, taps * chans, rows), BF16),
        vmem(layers, F32),
        vmem((3 * rows, taps * rows), BF16),
        vmem((taps * rows, 3 * rows), BF16),
        vmem((128, rows), jnp.int32),
        vmem((depth, chans, taps * chans), BF16),
        vmem((depth, taps * chans, chans), BF16),
        vmem((chans, rows), F32),
        vmem(layers, BF16),
        vmem(layers, BF16),
        vmem(layers, BF16),
        vmem(layers, BF16),
        vmem((width, 3 * rows), F32),
        vmem((width, rows), BF16),
        vmem((width, rows), BF16),
        vmem((width, rows), BF16),
        vmem((width, rows), BF16),
        vmem((width, rows), F32),
        vmem((width, rows), BF16),
        vmem((others, width, rows), BF16),
        vmem((others, width, chans), BF16),
        vmem((others, chans, rows), BF16),
        dma((depth, 2)), dma((depth, 2)), dma((depth, 2)), dma((depth, 2)),
        dma((2,)), dma((2,)), dma((3, others)), dma((3, others)),
    ]
    whole = pl.BlockSpec(memory_space=pltpu.VMEM)
    map_grad, tap_grads = pl.pallas_call(
        functools.partial(kernel, n_sky, n_branch),
        out_shape=(
            jax.ShapeDtypeStruct((chans, rows), BF16),
            jax.ShapeDtypeStruct((depth, taps, chans, chans), F32),
        ),
        in_specs=[whole] * 7,
        out_specs=(whole, whole),
        scratch_shapes=scratch,
        compiler_params=pltpu.CompilerParams(
            collective_id=0, has_side_effects=True, vmem_limit_bytes=48 * 1024 * 1024
        ),
        name="unet_backward",
    )(sky_maps[0], footprint, neighbours, enc_weight[0], join_weight, dec_weight, cotangent)
    normalizer = 1.0 / math.sqrt(rows * n_sky)
    summed = lax.psum(tap_grads, "sky") * normalizer
    return map_grad[None], summed[None]


def solution(mesh):
    in_specs = (
        P("branch", None, "sky"),
        P("branch", "sky"),
        P(None, "sky"),
        P("branch", None, None, None, None),
        P(None, "branch"),
        P(None, "branch", None),
        P("branch", "sky"),
    )
    out_specs = (P("branch", None, "sky"), P("branch", None, None, None, None))
    return jax.shard_map(
        functools.partial(per_device, mesh.shape["sky"], mesh.shape["branch"]),
        mesh=mesh, in_specs=in_specs, out_specs=out_specs, check_vma=False,
    )
```

profile of v0, /device:TPU:0, one launch (start us, length us, event | category | flops | bytes accessed | tf_op | source)
XLA Modules:
  0.0 171.8 jit_solution(10673771449299139432)
XLA Ops:
  7.2 0.0 all-reduce.2.cloned.1.call-start
  7.2 0.9 copy.9.join
  8.1 0.0 copy-start
  8.1 1.2 copy-done
  9.3 0.0 copy-start.1
  9.3 1.1 copy-done.1
  10.3 0.0 copy-start.2
  10.3 0.8 copy-done.2
  11.2 0.0 copy-start.3
  11.2 0.8 copy-done.3
  11.9 0.0 copy-start.4
  11.9 0.7 copy-done.4
  12.6 0.0 copy-start.5
  12.6 0.7 copy-done.5
  13.3 48.1 %unet_backward.1 = (bf16[64,256]{1,0:T(8,128)(2,1)S(1)}, f32[6,9,64,64]{3,2,1,0:T(8,128)}) custom-call(bf16[64,256]{1,0:T(8,128)(2,1)S(1)} %bitcast.6, s32[1,256]{1,0:T(1,128)S(1)} %copy-done.5, s32[9,256]{1,0:T(8,128)S(1)} %copy-done.4, bf16[6,9,64,64]{3,2,1,0:T(8,128)(2,1)S(1)} %bitcast.5, bf16[256,64]{1,0:T(8,128)(2,1)S(1)} %copy.9.join, ...), custom_call_target="tpu_custom_call" | custom-call | tf_op jit(solution)/shard_map/unet_backward/pallas_call | solution.py:308
  61.5 0.0 all-reduce.2.cloned.1.call-update
  61.5 100.0 %all-reduce.2.cloned.1.call-done = f32[6,9,64,64]{3,2,1,0:T(8,128)} async-done(((f32[6,9,64,64]{3,2,1,0:T(8,128)}), f32[6,9,64,64]{3,2,1,0:T(8,128)}) %all-reduce.2.cloned.1.call-update) | async-done | bytes 884752 | tf_op jit(solution)/shard_map/psum | solution.py:323
  161.5 2.9 %multiply_bitcast_fusion = f32[1,6,9,64,64]{4,3,2,1,0:T(8,128)} fusion(f32[6,9,64,64]{3,2,1,0:T(8,128)} %all-reduce.2.cloned.1.call-done), kind=kLoop, calls=%fused_computation | loop fusion | flops 221184 | bytes 1769472 | tf_op jit(solution)/shard_map/broadcast_in_dim | solution.py:324
  164.4 0.6 copy.12
Async XLA Ops:
  7.2 154.3 %all-reduce.2.cloned.1.call-start = ((), (), s32[]{:S(2)}) async-start(), calls=%async_computation | async-start | bytes 3538944 | tf_op jit(solution)/shard_map/psum | solution.py:323
  8.1 1.2 copy-start
  9.3 1.1 copy-start.1
  10.3 0.8 copy-start.2
  11.2 0.8 copy-start.3
  11.9 0.7 copy-start.4
  12.6 0.7 copy-start.5
Sparse Core Ops, SparseCore 0:
  61.6 99.8 all-reduce.1
where the time goes:
time: 172 us
  waiting for transfers between devices  100 us (58%)
  Pallas kernels  48.1 us (28%)
  between operations  14.1 us (8%)
  local copies, waits for them, and re-layouts  6.71 us (4%)
  other arithmetic  2.92 us (2%)
    psum x1, waiting for transfers between devices, per_device(): summed = lax.psum(tap_grads, 'sky') * normalizer  100 us
    pallas_call x1, Pallas kernels, per_device(): pl.pallas_call(functools.partial(kernel, n_sky, n_branch), out_shape=(jax...  48.1 us
    unnamed x14, local copies, waits for them, and re-layouts  6.71 us
  transfers between devices with their start and end apart: 1, of which 1 were waited for; matrix products, arithmetic and copies ran while one was open for 0% of the time, Pallas kernels for 0%

commit v1 on v0

--- a/solution.py
+++ b/solution.py
@@ -18,23 +18,46 @@
 
 
 def kernel(
-    n_sky, n_branch,
-    maps, foot, nb, enc, join, dec, cot,
+    n_sky, n_branch, near_group,
+    maps_in, foot_in, nb_in, enc_in, join_in, dec_in, cot_in,
     map_out, grad_out,
+    foot, nb, enc, join, dec, cot,
     own, from_left, from_right, picked, slope, one_hot, one_hot_t, rel, enc_flat, enc_t,
     grad, edge_left, edge_right, back_left, back_right,
     dec_acc, rim_left, rim_right, got_left, got_right, unit_own, unit_send, unit_got,
     join_got, top_got,
+    part_own, part_got, mid, final,
     fwd_send, fwd_recv, bwd_send, bwd_recv, rim_send, rim_recv, br_send, br_recv,
+    near_send, near_recv, far_send, far_recv, out_send, out_recv, local_sem,
 ):
     depth, taps = enc.shape[0], enc.shape[1]
-    chans, rows = maps.shape
+    chans, rows = maps_in.shape
+    far_group = n_sky // near_group
+    share = chans // near_group
     sky = lax.axis_index("sky")
     branch = lax.axis_index("branch")
     has_left, has_right = sky > 0, sky < n_sky - 1
     left, right = jnp.maximum(sky - 1, 0), jnp.minimum(sky + 1, n_sky - 1)
     peers = [(d, lax.rem(branch + d, n_branch)) for d in range(1, n_branch)]
 
+    mine = lax.rem(sky, near_group)
+    level = sky // near_group
+    mates = [
+        (d, sky - mine + lax.rem(mine + d, near_group)) for d in range(1, near_group)
+    ]
+    stack = [
+        (d, lax.rem(level + d, far_group) * near_group + mine) for d in range(1, far_group)
+    ]
+
+    sources = (maps_in, foot_in, nb_in, join_in, enc_in, dec_in, cot_in)
+    targets = (own.at[0], foot, nb, join, enc, dec, cot)
+    loads = [
+        pltpu.make_async_copy(src, dst, local_sem.at[i])
+        for i, (src, dst) in enumerate(zip(sources, targets))
+    ]
+    for load in loads:
+        load.start()
+
     barrier = pltpu.get_barrier_semaphore()
 
     @pl.when(has_left)
@@ -47,8 +70,12 @@
 
     for _, peer in peers:
         pl.semaphore_signal(barrier, inc=1, device_id={"branch": peer}, device_id_type=MESH)
+    for _, peer in mates + stack:
+        pl.semaphore_signal(barrier, inc=1, device_id={"sky": peer}, device_id_type=MESH)
     pl.semaphore_wait(
-        barrier, has_left.astype(jnp.int32) + has_right.astype(jnp.int32) + (n_branch - 1)
+        barrier,
+        has_left.astype(jnp.int32) + has_right.astype(jnp.int32)
+        + (n_branch - 1 + near_group - 1 + far_group - 1),
     )
 
     def to_left(src, dst, send, recv):
@@ -118,8 +145,68 @@
             for d, peer in peers
         ]
 
-    own[0] = maps[...]
+    def over_sky(peer, src, dst, send, recv):
+        return pltpu.make_async_remote_copy(
+            src_ref=src, dst_ref=dst, send_sem=send, recv_sem=recv,
+            device_id={"sky": peer}, device_id_type=MESH,
+        )
+
+    def scatter_copies(layer):
+        return [
+            over_sky(
+                peer, part_own.at[layer, lax.rem(mine + d, near_group)], part_got.at[layer, d - 1],
+                near_send.at[layer, d - 1], near_recv.at[layer, d - 1],
+            )
+            for d, peer in mates
+        ]
+
+    def level_copies(layer):
+        return [
+            over_sky(
+                peer, mid.at[layer, level], mid.at[layer, level],
+                far_send.at[layer, d - 1], far_recv.at[layer, d - 1],
+            )
+            for d, peer in stack
+        ]
+
+    def gather_copies(layer):
+        return [
+            over_sky(
+                peer, final.at[layer, mine], final.at[layer, mine],
+                out_send.at[layer, d - 1], out_recv.at[layer, d - 1],
+            )
+            for d, peer in mates
+        ]
+
+    def sum_near(layer):
+        total = part_own[layer, mine].astype(F32)
+        for i, copy in enumerate(scatter_copies(layer)):
+            copy.wait_recv()
+            total = total + part_got[layer, i].astype(F32)
+        mid[layer, level] = total.astype(BF16)
+        for copy in level_copies(layer):
+            copy.start()
+
+    def sum_far(layer):
+        for copy in level_copies(layer):
+            copy.wait_recv()
+        total = mid[layer, 0].astype(F32)
+        for z in range(1, far_group):
+            total = total + mid[layer, z].astype(F32)
+        final[layer, mine] = total.astype(BF16)
+        for copy in gather_copies(layer):
+            copy.start()
+
+    def finish(layer):
+        for copy in gather_copies(layer):
+            copy.wait_recv()
+        whole = jnp.concatenate([final[layer, i] for i in range(near_group)], axis=0)
+        for k in range(taps):
+            grad_out[layer, k] = whole[:, k * chans : (k + 1) * chans]
+
+    loads[0].wait()
     start(halo(0))
+    loads[3].wait()
     join_copies = across(join, join_got, 0)
     for copy in join_copies:
         copy.start()
@@ -136,6 +223,8 @@
         back_right[...] = jnp.zeros_like(back_right)
         got_right[...] = jnp.zeros_like(got_right)
 
+    loads[1].wait()
+    loads[2].wait()
     first = (sky - 1) * rows
     near = nb[...]
     offset = jnp.where(near >= 0, near - first, -1)
@@ -157,6 +246,8 @@
                 col[:, k : k + 1] == index, 1.0, 0.0
             ).astype(BF16)
 
+    for load in loads[4:]:
+        load.wait()
     retained = foot[...].astype(F32)
     dec_acc[...] = jnp.zeros_like(dec_acc)
     dec_steps = 3
@@ -219,7 +310,7 @@
     top_copies = across(own.at[depth], top_got, 2)
     for copy in top_copies:
         copy.start()
-    joined = matmul(join[...], own[depth])
+    joined = matmul(join[...], own[depth], ((0,), (0,)))
     for copy in join_copies:
         copy.wait_recv()
     unit_copies = across(unit_send, unit_got, 1)
@@ -229,11 +320,11 @@
         unit = unit + unit_got[i].astype(F32)
     for i, copy in enumerate(top_copies):
         copy.wait_recv()
-        joined = joined + matmul(join_got[i], top_got[i])
+        joined = joined + matmul(join_got[i], top_got[i], ((0,), (0,)))
     sig = jax.nn.sigmoid(joined)
     unit_slope = (sig * (1.0 + joined * (1.0 - sig))).astype(BF16).astype(F32)
     unit_grad = (unit * unit_slope).astype(BF16)
-    grad[...] = matmul(join[...], unit_grad, ((0,), (0,)))
+    grad[...] = matmul(join[...], unit_grad)
 
     @pl.loop(0, depth)
     def backward(step):
@@ -250,17 +341,40 @@
         start(back(layer))
         inner = masked + matmul(terms, one_hot_t[:, 0:rows])
         weight = matmul(act, picked[layer], ((1,), (1,)))
-        for k in range(taps):
-            grad_out[layer, k] = weight[:, k * chans : (k + 1) * chans]
+        for i in range(near_group):
+            part_own[layer, i] = weight[i * share : (i + 1) * share].astype(BF16)
+        for copy in scatter_copies(layer):
+            copy.start()
+
+        @pl.when(step >= 1)
+        def _():
+            sum_near(layer + 1)
+
+        @pl.when(step >= 2)
+        def _():
+            sum_far(layer + 2)
+
+        @pl.when(step >= 3)
+        def _():
+            finish(layer + 3)
+
         wait_recv(back(layer))
         grad[...] = inner + back_left[layer].astype(F32) + back_right[layer].astype(F32)
 
     map_out[...] = grad[...].astype(BF16)
+    sum_near(0)
+    sum_far(1)
+    finish(2)
+    sum_far(0)
+    finish(1)
+    finish(0)
 
     @pl.loop(0, depth)
     def drain(layer):
         wait_send(halo(layer))
         wait_send(back(layer))
+        for copy in scatter_copies(layer) + level_copies(layer) + gather_copies(layer):
+            copy.wait_send()
 
     wait_send(rims())
     for copy in join_copies + unit_copies + top_copies:
@@ -272,10 +386,20 @@
     depth, taps = enc_weight.shape[1:3]
     width = dec_weight.shape[2]
     others = max(n_branch - 1, 1)
+    near_group = math.gcd(n_sky, 4)
+    far_group = n_sky // near_group
+    share = chans // near_group
+    near, far = max(near_group - 1, 1), max(far_group - 1, 1)
     vmem = pltpu.VMEM
     dma = pltpu.SemaphoreType.DMA
     layers = (depth, chans, rows)
     scratch = [
+        vmem(footprint.shape, jnp.int32),
+        vmem(neighbours.shape, jnp.int32),
+        vmem(enc_weight.shape[1:], BF16),
+        vmem((chans, width), BF16),
+        vmem(dec_weight.shape, BF16),
+        vmem(cotangent.shape, BF16),
         vmem((depth + 1, chans, rows), BF16),
         vmem(layers, BF16),
         vmem(layers, BF16),
@@ -299,28 +423,34 @@
         vmem((width, rows), F32),
         vmem((width, rows), BF16),
         vmem((others, width, rows), BF16),
-        vmem((others, width, chans), BF16),
+        vmem((others, chans, width), BF16),
         vmem((others, chans, rows), BF16),
+        vmem((depth, near_group, share, taps * chans), BF16),
+        vmem((depth, near, share, taps * chans), BF16),
+        vmem((depth, far_group, share, taps * chans), BF16),
+        vmem((depth, near_group, share, taps * chans), BF16),
         dma((depth, 2)), dma((depth, 2)), dma((depth, 2)), dma((depth, 2)),
         dma((2,)), dma((2,)), dma((3, others)), dma((3, others)),
+        dma((depth, near)), dma((depth, near)), dma((depth, far)), dma((depth, far)),
+        dma((depth, near)), dma((depth, near)), dma((7,)),
     ]
     whole = pl.BlockSpec(memory_space=pltpu.VMEM)
     map_grad, tap_grads = pl.pallas_call(
-        functools.partial(kernel, n_sky, n_branch),
+        functools.partial(kernel, n_sky, n_branch, near_group),
         out_shape=(
             jax.ShapeDtypeStruct((chans, rows), BF16),
-            jax.ShapeDtypeStruct((depth, taps, chans, chans), F32),
+            jax.ShapeDtypeStruct((depth, taps, chans, chans), BF16),
         ),
-        in_specs=[whole] * 7,
+        in_specs=[pl.BlockSpec(memory_space=pltpu.HBM)] * 7,
         out_specs=(whole, whole),
         scratch_shapes=scratch,
         compiler_params=pltpu.CompilerParams(
-            collective_id=0, has_side_effects=True, vmem_limit_bytes=48 * 1024 * 1024
+            collective_id=0, has_side_effects=True, vmem_limit_bytes=60 * 1024 * 1024
         ),
         name="unet_backward",
-    )(sky_maps[0], footprint, neighbours, enc_weight[0], join_weight, dec_weight, cotangent)
+    )(sky_maps[0], footprint, neighbours, enc_weight[0], join_weight.T, dec_weight, cotangent)
     normalizer = 1.0 / math.sqrt(rows * n_sky)
-    summed = lax.psum(tap_grads, "sky") * normalizer
+    summed = tap_grads.astype(F32) * normalizer
     return map_grad[None], summed[None]
 
 

time: 172 us -> 65.6 us (0.38)
  waiting for transfers between devices: 100 us -> 0 us
  between operations: 14.1 us -> 0.65 us
  Pallas kernels: 48.1 us -> 61.5 us
  local copies, waits for them, and re-layouts: 6.71 us -> 0.62 us
    psum x1 -> x0, waiting for transfers between devices: 100 us -> none  [per_device(): summed = lax.psum(tap_grads, 'sky') * normalizer]
    pallas_call x1, Pallas kernels: 48.1 us -> 61.5 us  [per_device(): pl.pallas_call(functools.partial(kernel, n_sky, n_branch, near_group), ou...]
    unnamed x14 -> x3, local copies, waits for them, and re-layouts: 6.71 us -> 0.62 us
  transfers between devices with their start and end apart: 1 -> 0, of which waited for: 1 -> 0; matrix products, arithmetic and copies ran while one was open for 0% -> 0% of each run, Pallas kernels for 0% -> 0%
where the time goes in v1:
time: 65.6 us; the launch traced here: 65.4 us
  Pallas kernels  61.5 us (94%)
  other arithmetic  2.6 us (4%)
    pallas_call x1, Pallas kernels, per_device(): pl.pallas_call(functools.partial(kernel, n_sky, n_branch, near_group), ou...  61.5 us
    broadcast_in_dim x1, other arithmetic, per_device(): return (map_grad[None], summed[None])  2.6 us

profile of v1, /device:TPU:0, one launch (start us, length us, event | category | flops | bytes accessed | tf_op | source)
XLA Modules:
  0.0 65.4 jit_solution(7507730789722116763)
XLA Ops:
  0.6 61.5 %unet_backward.1 = (bf16[64,256]{1,0:T(8,128)(2,1)}, bf16[6,9,64,64]{3,2,1,0:T(8,128)(2,1)}) custom-call(bf16[64,256]{1,0:T(8,128)(2,1)} %bitcast.7, s32[1,256]{1,0:T(1,128)} %foot_in.1, s32[9,256]{1,0:T(8,128)} %nb_in.1, bf16[6,9,64,64]{3,2,1,0:T(8,128)(2,1)} %bitcast.6, bf16[64,256]{1,0:T(8,128)(2,1)} %bitcast.8, bf16[9,128,256]{2,1,0:T(8,128)(2,1)} %dec_in.1, ...), custom_call_target="tpu_custom_call" | custom-call | tf_op jit(solution)/shard_map/unet_backward/pallas_call | solution.py:438
  62.2 0.0 copy-start
  62.2 2.6 %multiply_bitcast_fusion = f32[1,6,9,64,64]{4,3,2,1,0:T(8,128)} fusion(bf16[6,9,64,64]{3,2,1,0:T(8,128)(2,1)} %get-tuple-element.5), kind=kLoop, calls=%fused_computation | loop fusion | flops 442368 | bytes 1327104 | tf_op jit(solution)/shard_map/broadcast_in_dim | solution.py:454
  64.8 0.0 copy-done
  64.8 0.6 copy.10
Async XLA Ops:
  62.2 2.6 %copy-start = (bf16[64,256]{1,0:T(8,128)(2,1)S(1)}, bf16[64,256]{1,0:T(8,128)(2,1)}, u32[]{:S(2)}) copy-start(bf16[64,256]{1,0:T(8,128)(2,1)} %get-tuple-element.4) | copy-start | bytes 98308

commit v2 on v1

--- a/solution.py
+++ b/solution.py
@@ -22,13 +22,13 @@
     maps_in, foot_in, nb_in, enc_in, join_in, dec_in, cot_in,
     map_out, grad_out,
     foot, nb, enc, join, dec, cot,
-    own, from_left, from_right, picked, slope, one_hot, one_hot_t, rel, enc_flat, enc_t,
-    grad, edge_left, edge_right, back_left, back_right,
+    own, from_side, picked, slope, one_hot, one_hot_t, rel, turned, enc_flat, enc_t,
+    grad, edge, back_side, staged, map_own,
     dec_acc, rim_left, rim_right, got_left, got_right, unit_own, unit_send, unit_got,
     join_got, top_got,
     part_own, part_got, mid, final,
     fwd_send, fwd_recv, bwd_send, bwd_recv, rim_send, rim_recv, br_send, br_recv,
-    near_send, near_recv, far_send, far_recv, out_send, out_recv, local_sem,
+    near_send, near_recv, far_send, far_recv, out_send, out_recv, local_sem, store_sem,
 ):
     depth, taps = enc.shape[0], enc.shape[1]
     chans, rows = maps_in.shape
@@ -92,14 +92,14 @@
 
     def halo(layer):
         return (
-            to_left(own.at[layer], from_right.at[layer], fwd_send.at[layer, 0], fwd_recv.at[layer, 0]),
-            to_right(own.at[layer], from_left.at[layer], fwd_send.at[layer, 1], fwd_recv.at[layer, 1]),
+            to_left(own.at[layer], from_side.at[1, layer], fwd_send.at[layer, 0], fwd_recv.at[layer, 0]),
+            to_right(own.at[layer], from_side.at[0, layer], fwd_send.at[layer, 1], fwd_recv.at[layer, 1]),
         )
 
     def back(layer):
         return (
-            to_left(edge_left.at[layer], back_right.at[layer], bwd_send.at[layer, 0], bwd_recv.at[layer, 0]),
-            to_right(edge_right.at[layer], back_left.at[layer], bwd_send.at[layer, 1], bwd_recv.at[layer, 1]),
+            to_left(edge.at[0, layer], back_side.at[1, layer], bwd_send.at[layer, 0], bwd_recv.at[layer, 0]),
+            to_right(edge.at[1, layer], back_side.at[0, layer], bwd_send.at[layer, 1], bwd_recv.at[layer, 1]),
         )
 
     def rims():
@@ -125,6 +125,27 @@
         @pl.when(has_left)
         def _():
             pair[1].wait_recv()
+
+    def wait_recv_side(pair, side):
+        @pl.when(jnp.logical_and(side == 1, has_right))
+        def _():
+            pair[0].wait_recv()
+
+        @pl.when(jnp.logical_and(side == 0, has_left))
+        def _():
+            pair[1].wait_recv()
+
+    def start_side(pair, side):
+        @pl.when(jnp.logical_and(side == 0, has_left))
+        def _():
+            pair[0].start()
+
+        @pl.when(jnp.logical_and(side == 1, has_right))
+        def _():
+            pair[1].start()
+
+    close = 1 - lax.rem(sky, 2)
+    distant = 1 - close
 
     def wait_send(pair):
         @pl.when(has_left)
@@ -197,12 +218,16 @@
         for copy in gather_copies(layer):
             copy.start()
 
+    def store(layer):
+        return pltpu.make_async_copy(staged.at[layer], grad_out.at[layer], store_sem.at[layer])
+
     def finish(layer):
         for copy in gather_copies(layer):
             copy.wait_recv()
         whole = jnp.concatenate([final[layer, i] for i in range(near_group)], axis=0)
         for k in range(taps):
-            grad_out[layer, k] = whole[:, k * chans : (k + 1) * chans]
+            staged[layer, k] = whole[:, k * chans : (k + 1) * chans]
+        store(layer).start()
 
     loads[0].wait()
     start(halo(0))
@@ -213,14 +238,14 @@
 
     @pl.when(jnp.logical_not(has_left))
     def _():
-        from_left[...] = jnp.zeros_like(from_left)
-        back_left[...] = jnp.zeros_like(back_left)
+        from_side[0] = jnp.zeros(from_side.shape[1:], BF16)
+        back_side[0] = jnp.zeros(back_side.shape[1:], BF16)
         got_left[...] = jnp.zeros_like(got_left)
 
     @pl.when(jnp.logical_not(has_right))
     def _():
-        from_right[...] = jnp.zeros_like(from_right)
-        back_right[...] = jnp.zeros_like(back_right)
+        from_side[1] = jnp.zeros(from_side.shape[1:], BF16)
+        back_side[1] = jnp.zeros(back_side.shape[1:], BF16)
         got_right[...] = jnp.zeros_like(got_right)
 
     loads[1].wait()
@@ -235,17 +260,13 @@
     rel[...] = jnp.full(rel.shape, -1, jnp.int32)
     rel[0:taps, :] = part
     col = jnp.transpose(rel[...])
+    turned[...] = col
     for k in range(taps):
         lanes = slice(k * rows, (k + 1) * rows)
         line = rel[k : k + 1, :]
         for p in range(3):
             index = lax.broadcasted_iota(jnp.int32, (rows, rows), 0) + p * rows
             one_hot[p * rows : (p + 1) * rows, lanes] = jnp.where(line == index, 1.0, 0.0).astype(BF16)
-            index = lax.broadcasted_iota(jnp.int32, (rows, rows), 1) + p * rows
-            one_hot_t[lanes, p * rows : (p + 1) * rows] = jnp.where(
-                col[:, k : k + 1] == index, 1.0, 0.0
-            ).astype(BF16)
-
     for load in loads[4:]:
         load.wait()
     retained = foot[...].astype(F32)
@@ -263,39 +284,48 @@
             enc_flat[layer, :, k * chans : (k + 1) * chans] = tap
             enc_t[layer, k * chans : (k + 1) * chans, :] = jnp.transpose(tap)
 
-        @pl.when(layer < dec_steps)
-        def _():
+        def decode(step):
             each = taps // dec_steps
             parts = []
-            for j in range(each):
-                term = matmul(dec[layer * each + j], cot[...], ((0,), (0,)))
-                parts.append(term.astype(BF16))
-            span = each * rows
-            table = one_hot_t[pl.ds(pl.multiple_of(layer * span, span), span), :]
-            dec_acc[...] += matmul(jnp.concatenate(parts, axis=1), table)
+            for k in range(step * each, (step + 1) * each):
+                line = turned[:, k : k + 1]
+                for p in range(3):
+                    index = lax.broadcasted_iota(jnp.int32, (rows, rows), 1) + p * rows
+                    one_hot_t[p, k * rows : (k + 1) * rows, :] = jnp.where(
+                        line == index, 1.0, 0.0
+                    ).astype(BF16)
+                parts.append(matmul(dec[k], cot[...], ((0,), (0,))).astype(BF16))
+            terms = jnp.concatenate(parts, axis=1)
+            span = slice(step * each * rows, (step + 1) * each * rows)
+            for p in range(3):
+                dec_acc[p] = dec_acc[p] + matmul(terms, one_hot_t[p, span, :])
+
+        for step in range(dec_steps):
+            pl.when(layer == step)(functools.partial(decode, step))
 
         @pl.when(layer == dec_steps)
         def _():
-            rim_left[...] = dec_acc[:, rows : 2 * rows].astype(BF16)
-            rim_right[...] = dec_acc[:, 2 * rows : 3 * rows].astype(BF16)
+            rim_left[...] = dec_acc[1].astype(BF16)
+            rim_right[...] = dec_acc[2].astype(BF16)
             start(rims())
 
         @pl.when(layer == dec_steps + 1)
         def _():
             wait_recv(rims())
-            total = dec_acc[:, 0:rows] + got_left[...].astype(F32) + got_right[...].astype(F32)
+            total = dec_acc[0] + got_left[...].astype(F32) + got_right[...].astype(F32)
             unit_own[...] = total
             unit_send[...] = total.astype(BF16)
             for copy in across(unit_send, unit_got, 1):
                 copy.start()
 
-        wait_recv(halo(layer))
-        for k in range(taps):
-            lanes = slice(k * rows, (k + 1) * rows)
-            both = jnp.concatenate([from_left[layer], from_right[layer]], axis=1)
-            block = matmul(both, one_hot[rows : 3 * rows, lanes])
-            at = slice(k * chans, (k + 1) * chans)
-            picked[layer, at, :] = picked[layer, at, :] + block.astype(BF16)
+        for side in (close, distant):
+            wait_recv_side(halo(layer), side)
+            arrived = from_side[side, layer]
+            table = pl.ds(pl.multiple_of((1 + side) * rows, rows), rows)
+            for k in range(taps):
+                block = matmul(arrived, one_hot[table, k * rows : (k + 1) * rows])
+                at = slice(k * chans, (k + 1) * chans)
+                picked[layer, at, :] = picked[layer, at, :] + block.astype(BF16)
         pre = matmul(enc_flat[layer], picked[layer])
         sig = jax.nn.sigmoid(pre)
         after = retained * (hidden.astype(F32) + pre * sig)
@@ -326,26 +356,35 @@
     unit_grad = (unit * unit_slope).astype(BF16)
     grad[...] = matmul(join[...], unit_grad)
 
-    @pl.loop(0, depth)
-    def backward(step):
-        layer = depth - 1 - step
-        masked = retained * grad[...]
-        act = (masked * slope[layer]).astype(BF16)
-        terms = matmul(enc_t[layer], act).astype(BF16)
-        terms = jnp.concatenate(
-            [terms[k * chans : (k + 1) * chans] for k in range(taps)], axis=1
-        )
-        edge = matmul(terms, one_hot_t[:, rows : 3 * rows]).astype(BF16)
-        edge_left[layer] = edge[:, :rows]
-        edge_right[layer] = edge[:, rows:]
-        start(back(layer))
-        inner = masked + matmul(terms, one_hot_t[:, 0:rows])
+    def weigh(layer, act):
         weight = matmul(act, picked[layer], ((1,), (1,)))
         for i in range(near_group):
             part_own[layer, i] = weight[i * share : (i + 1) * share].astype(BF16)
         for copy in scatter_copies(layer):
             copy.start()
 
+    def spread(layer, act):
+        terms = matmul(enc_t[layer], act).astype(BF16)
+        terms = jnp.concatenate(
+            [terms[k * chans : (k + 1) * chans] for k in range(taps)], axis=1
+        )
+        for side in (distant, close):
+            edge[side, layer] = matmul(terms, one_hot_t[1 + side]).astype(BF16)
+            start_side(back(layer), side)
+        return matmul(terms, one_hot_t[0])
+
+    def take_back(layer, inner):
+        wait_recv(back(layer))
+        return inner + back_side[0, layer].astype(F32) + back_side[1, layer].astype(F32)
+
+    @pl.loop(0, depth - 1)
+    def backward(step):
+        layer = depth - 1 - step
+        masked = retained * grad[...]
+        act = (masked * slope[layer]).astype(BF16)
+        inner = masked + spread(layer, act)
+        weigh(layer, act)
+
         @pl.when(step >= 1)
         def _():
             sum_near(layer + 1)
@@ -358,27 +397,60 @@
         def _():
             finish(layer + 3)
 
-        wait_recv(back(layer))
-        grad[...] = inner + back_left[layer].astype(F32) + back_right[layer].astype(F32)
-
-    map_out[...] = grad[...].astype(BF16)
+        grad[...] = take_back(layer, inner)
+
+    masked = retained * grad[...]
+    act = (masked * slope[0]).astype(BF16)
+    weigh(0, act)
+    inner = masked + spread(0, act)
+    late = [k for k in (1, 2, 3) if k < depth]
+    for k, stage in zip(late, (sum_near, sum_far, finish)):
+        stage(k)
     sum_near(0)
-    sum_far(1)
-    finish(2)
+    if depth > 1:
+        sum_far(1)
+    if depth > 2:
+        finish(2)
+    map_own[...] = take_back(0, inner).astype(BF16)
+    map_copy = pltpu.make_async_copy(map_own, map_out, local_sem.at[0])
+    map_copy.start()
     sum_far(0)
-    finish(1)
+    if depth > 1:
+        finish(1)
     finish(0)
+    map_copy.wait()
 
     @pl.loop(0, depth)
     def drain(layer):
         wait_send(halo(layer))
         wait_send(back(layer))
+        store(layer).wait()
         for copy in scatter_copies(layer) + level_copies(layer) + gather_copies(layer):
             copy.wait_send()
 
     wait_send(rims())
     for copy in join_copies + unit_copies + top_copies:
         copy.wait_send()
+
+
+def scale_kernel(normalizer, map_in, sums_in, map_out, sums_out, held, sums, scaled, in_sem, out_sem):
+    depth = sums_in.shape[0]
+    reads = [pltpu.make_async_copy(sums_in.at[i], sums.at[i], in_sem.at[i]) for i in range(depth)]
+    writes = [
+        pltpu.make_async_copy(scaled.at[i], sums_out.at[i], out_sem.at[i]) for i in range(depth)
+    ]
+    reads.append(pltpu.make_async_copy(map_in, held, in_sem.at[depth]))
+    writes.append(pltpu.make_async_copy(held, map_out, out_sem.at[depth]))
+    for read in reads:
+        read.start()
+    for i in range(depth):
+        reads[i].wait()
+        scaled[i] = sums[i].astype(F32) * normalizer
+        writes[i].start()
+    reads[depth].wait()
+    writes[depth].start()
+    for write in writes:
+        write.wait()
 
 
 def per_device(n_sky, n_branch, sky_maps, footprint, neighbours, enc_weight, join_weight, dec_weight, cotangent):
@@ -401,21 +473,21 @@
         vmem(dec_weight.shape, BF16),
         vmem(cotangent.shape, BF16),
         vmem((depth + 1, chans, rows), BF16),
-        vmem(layers, BF16),
-        vmem(layers, BF16),
+        vmem((2,) + layers, BF16),
         vmem((depth, taps * chans, rows), BF16),
         vmem(layers, F32),
         vmem((3 * rows, taps * rows), BF16),
-        vmem((taps * rows, 3 * rows), BF16),
+        vmem((3, taps * rows, rows), BF16),
         vmem((128, rows), jnp.int32),
+        vmem((rows, 128), jnp.int32),
         vmem((depth, chans, taps * chans), BF16),
         vmem((depth, taps * chans, chans), BF16),
         vmem((chans, rows), F32),
-        vmem(layers, BF16),
-        vmem(layers, BF16),
-        vmem(layers, BF16),
-        vmem(layers, BF16),
-        vmem((width, 3 * rows), F32),
+        vmem((2,) + layers, BF16),
+        vmem((2,) + layers, BF16),
+        vmem((depth, taps, chans, chans), BF16),
+        vmem((chans, rows), BF16),
+        vmem((3, width, rows), F32),
         vmem((width, rows), BF16),
         vmem((width, rows), BF16),
         vmem((width, rows), BF16),
@@ -432,17 +504,17 @@
         dma((depth, 2)), dma((depth, 2)), dma((depth, 2)), dma((depth, 2)),
         dma((2,)), dma((2,)), dma((3, others)), dma((3, others)),
         dma((depth, near)), dma((depth, near)), dma((depth, far)), dma((depth, far)),
-        dma((depth, near)), dma((depth, near)), dma((7,)),
+        dma((depth, near)), dma((depth, near)), dma((7,)), dma((depth,)),
     ]
-    whole = pl.BlockSpec(memory_space=pltpu.VMEM)
+    hbm = pl.BlockSpec(memory_space=pltpu.HBM)
     map_grad, tap_grads = pl.pallas_call(
         functools.partial(kernel, n_sky, n_branch, near_group),
         out_shape=(
             jax.ShapeDtypeStruct((chans, rows), BF16),
             jax.ShapeDtypeStruct((depth, taps, chans, chans), BF16),
         ),
-        in_specs=[pl.BlockSpec(memory_space=pltpu.HBM)] * 7,
-        out_specs=(whole, whole),
+        in_specs=[hbm] * 7,
+        out_specs=(hbm, hbm),
         scratch_shapes=scratch,
         compiler_params=pltpu.CompilerParams(
             collective_id=0, has_side_effects=True, vmem_limit_bytes=60 * 1024 * 1024
@@ -450,7 +522,24 @@
         name="unet_backward",
     )(sky_maps[0], footprint, neighbours, enc_weight[0], join_weight.T, dec_weight, cotangent)
     normalizer = 1.0 / math.sqrt(rows * n_sky)
-    summed = tap_grads.astype(F32) * normalizer
+    map_grad, summed = pl.pallas_call(
+        functools.partial(scale_kernel, normalizer),
+        out_shape=(
+            jax.ShapeDtypeStruct((chans, rows), BF16),
+            jax.ShapeDtypeStruct((depth, taps, chans, chans), F32),
+        ),
+        in_specs=[hbm] * 2,
+        out_specs=(hbm, hbm),
+        scratch_shapes=[
+            vmem((chans, rows), BF16),
+            vmem((depth, taps, chans, chans), BF16),
+            vmem((depth, taps, chans, chans), F32),
+            dma((depth + 1,)),
+            dma((depth + 1,)),
+        ],
+        compiler_params=pltpu.CompilerParams(vmem_limit_bytes=60 * 1024 * 1024),
+        name="scale_sums",
+    )(map_grad, tap_grads)
     return map_grad[None], summed[None]
 
 

time: 65.6 us -> 62.1 us (0.947)
  other arithmetic: 2.6 us -> 0 us
    broadcast_in_dim x1 -> x0, other arithmetic: 2.6 us -> none  [per_device(): return (map_grad[None], summed[None])]
    pallas_call x1, Pallas kernels: 61.5 us -> 59 us  [per_device(): pl.pallas_call(functools.partial(kernel, n_sky, n_branch, near_group), ou...]
    pallas_call x0 -> x1, Pallas kernels: none -> 2.26 us  [per_device(): pl.pallas_call(functools.partial(scale_kernel, normalizer), out_shape=(ja...]
where the time goes in v2:
time: 62.1 us; the launch traced here: 61.9 us
  Pallas kernels  61.3 us (99%)
  between operations  0.64 us (1%)
    pallas_call x1, Pallas kernels, per_device(): pl.pallas_call(functools.partial(kernel, n_sky, n_branch, near_group), ou...  59 us
    pallas_call x1, Pallas kernels, per_device(): pl.pallas_call(functools.partial(scale_kernel, normalizer), out_shape=(ja...  2.26 us

profile of v2, /device:TPU:0, one launch (start us, length us, event | category | flops | bytes accessed | tf_op | source)
XLA Modules:
  0.0 61.9 jit_solution(15509758845502667551)
XLA Ops:
  0.6 59.0 %unet_backward.1 = (bf16[64,256]{1,0:T(8,128)(2,1)}, bf16[6,9,64,64]{3,2,1,0:T(8,128)(2,1)}) custom-call(bf16[64,256]{1,0:T(8,128)(2,1)} %bitcast.6, s32[1,256]{1,0:T(1,128)} %foot_in.1, s32[9,256]{1,0:T(8,128)} %nb_in.1, bf16[6,9,64,64]{3,2,1,0:T(8,128)(2,1)} %bitcast.5, bf16[64,256]{1,0:T(8,128)(2,1)} %bitcast.7, bf16[9,128,256]{2,1,0:T(8,128)(2,1)} %dec_in.1, ...), custom_call_target="tpu_custom_call" | custom-call | tf_op jit(solution)/shard_map/unet_backward/pallas_call | solution.py:510
  59.7 2.3 %scale_sums.1 = (bf16[64,256]{1,0:T(8,128)(2,1)}, f32[6,9,64,64]{3,2,1,0:T(8,128)}) custom-call(bf16[64,256]{1,0:T(8,128)(2,1)} %get-tuple-element.6.map_in, bf16[6,9,64,64]{3,2,1,0:T(8,128)(2,1)} %get-tuple-element.7.sums_in), custom_call_target="tpu_custom_call" | custom-call | tf_op jit(solution)/shard_map/scale_sums/pallas_call | solution.py:525

commit v3 on v2

--- a/solution.py
+++ b/solution.py
@@ -271,7 +271,8 @@
         load.wait()
     retained = foot[...].astype(F32)
     dec_acc[...] = jnp.zeros_like(dec_acc)
-    dec_steps = 3
+    dec_cuts = [0, taps // 9, 4 * taps // 9, 7 * taps // 9, taps]
+    dec_steps = len(dec_cuts) - 1
 
     @pl.loop(0, depth)
     def forward(layer):
@@ -282,12 +283,12 @@
         for k in range(taps):
             tap = enc[layer, k]
             enc_flat[layer, :, k * chans : (k + 1) * chans] = tap
-            enc_t[layer, k * chans : (k + 1) * chans, :] = jnp.transpose(tap)
+            enc_t[layer, :, k * chans : (k + 1) * chans] = jnp.transpose(tap)
 
         def decode(step):
-            each = taps // dec_steps
+            low, high = dec_cuts[step], dec_cuts[step + 1]
             parts = []
-            for k in range(step * each, (step + 1) * each):
+            for k in range(low, high):
                 line = turned[:, k : k + 1]
                 for p in range(3):
                     index = lax.broadcasted_iota(jnp.int32, (rows, rows), 1) + p * rows
@@ -296,7 +297,7 @@
                     ).astype(BF16)
                 parts.append(matmul(dec[k], cot[...], ((0,), (0,))).astype(BF16))
             terms = jnp.concatenate(parts, axis=1)
-            span = slice(step * each * rows, (step + 1) * each * rows)
+            span = slice(low * rows, high * rows)
             for p in range(3):
                 dec_acc[p] = dec_acc[p] + matmul(terms, one_hot_t[p, span, :])
 
@@ -364,14 +365,17 @@
             copy.start()
 
     def spread(layer, act):
-        terms = matmul(enc_t[layer], act).astype(BF16)
-        terms = jnp.concatenate(
-            [terms[k * chans : (k + 1) * chans] for k in range(taps)], axis=1
-        )
+        def placed(part):
+            spots = [
+                matmul(act, one_hot_t[part, k * rows : (k + 1) * rows, :]).astype(BF16)
+                for k in range(taps)
+            ]
+            return matmul(enc_t[layer], jnp.concatenate(spots, axis=0))
+
         for side in (distant, close):
-            edge[side, layer] = matmul(terms, one_hot_t[1 + side]).astype(BF16)
+            edge[side, layer] = placed(1 + side).astype(BF16)
             start_side(back(layer), side)
-        return matmul(terms, one_hot_t[0])
+        return placed(0)
 
     def take_back(layer, inner):
         wait_recv(back(layer))
@@ -389,13 +393,9 @@
         def _():
             sum_near(layer + 1)
 
-        @pl.when(step >= 2)
-        def _():
-            sum_far(layer + 2)
-
         @pl.when(step >= 3)
         def _():
-            finish(layer + 3)
+            sum_far(layer + 3)
 
         grad[...] = take_back(layer, inner)
 
@@ -403,17 +403,23 @@
     act = (masked * slope[0]).astype(BF16)
     weigh(0, act)
     inner = masked + spread(0, act)
-    late = [k for k in (1, 2, 3) if k < depth]
-    for k, stage in zip(late, (sum_near, sum_far, finish)):
-        stage(k)
+    if depth > 1:
+        sum_near(1)
+    for k in (3, 2):
+        if k < depth:
+            sum_far(k)
     sum_near(0)
+    for k in (5, 4):
+        if k < depth:
+            finish(k)
     if depth > 1:
         sum_far(1)
-    if depth > 2:
-        finish(2)
     map_own[...] = take_back(0, inner).astype(BF16)
     map_copy = pltpu.make_async_copy(map_own, map_out, local_sem.at[0])
     map_copy.start()
+    for k in (3, 2):
+        if k < depth:
+            finish(k)
     sum_far(0)
     if depth > 1:
         finish(1)
@@ -481,7 +487,7 @@
         vmem((128, rows), jnp.int32),
         vmem((rows, 128), jnp.int32),
         vmem((depth, chans, taps * chans), BF16),
-        vmem((depth, taps * chans, chans), BF16),
+        vmem((depth, chans, taps * chans), BF16),
         vmem((chans, rows), F32),
         vmem((2,) + layers, BF16),
         vmem((2,) + layers, BF16),

time: 62.1 us -> 62.5 us (level)
  no operation moved by 1% of the time
where the time goes in v3:
time: 62.5 us; the launch traced here: 62.4 us
  Pallas kernels  61.7 us (99%)
  between operations  0.64 us (1%)
    pallas_call x1, Pallas kernels, per_device(): pl.pallas_call(functools.partial(kernel, n_sky, n_branch, near_group), ou...  59.5 us
    pallas_call x1, Pallas kernels, per_device(): pl.pallas_call(functools.partial(scale_kernel, normalizer), out_shape=(ja...  2.26 us

profile of v3, /device:TPU:0, one launch (start us, length us, event | category | flops | bytes accessed | tf_op | source)
XLA Modules:
  0.0 62.4 jit_solution(3946963504743773982)
XLA Ops:
  0.6 59.5 %unet_backward.1 = (bf16[64,256]{1,0:T(8,128)(2,1)}, bf16[6,9,64,64]{3,2,1,0:T(8,128)(2,1)}) custom-call(bf16[64,256]{1,0:T(8,128)(2,1)} %bitcast.6, s32[1,256]{1,0:T(1,128)} %foot_in.1, s32[9,256]{1,0:T(8,128)} %nb_in.1, bf16[6,9,64,64]{3,2,1,0:T(8,128)(2,1)} %bitcast.5, bf16[64,256]{1,0:T(8,128)(2,1)} %bitcast.7, bf16[9,128,256]{2,1,0:T(8,128)(2,1)} %dec_in.1, ...), custom_call_target="tpu_custom_call" | custom-call | tf_op jit(solution)/shard_map/unet_backward/pallas_call | solution.py:516
  60.1 2.3 %scale_sums.1 = (bf16[64,256]{1,0:T(8,128)(2,1)}, f32[6,9,64,64]{3,2,1,0:T(8,128)}) custom-call(bf16[64,256]{1,0:T(8,128)(2,1)} %get-tuple-element.6.map_in, bf16[6,9,64,64]{3,2,1,0:T(8,128)(2,1)} %get-tuple-element.7.sums_in), custom_call_target="tpu_custom_call" | custom-call | tf_op jit(solution)/shard_map/scale_sums/pallas_call | solution.py:531

commit v4 on v3

--- a/solution.py
+++ b/solution.py
@@ -72,12 +72,6 @@
         pl.semaphore_signal(barrier, inc=1, device_id={"branch": peer}, device_id_type=MESH)
     for _, peer in mates + stack:
         pl.semaphore_signal(barrier, inc=1, device_id={"sky": peer}, device_id_type=MESH)
-    pl.semaphore_wait(
-        barrier,
-        has_left.astype(jnp.int32) + has_right.astype(jnp.int32)
-        + (n_branch - 1 + near_group - 1 + far_group - 1),
-    )
-
     def to_left(src, dst, send, recv):
         return pltpu.make_async_remote_copy(
             src_ref=src, dst_ref=dst, send_sem=send, recv_sem=recv,
@@ -228,13 +222,6 @@
         for k in range(taps):
             staged[layer, k] = whole[:, k * chans : (k + 1) * chans]
         store(layer).start()
-
-    loads[0].wait()
-    start(halo(0))
-    loads[3].wait()
-    join_copies = across(join, join_got, 0)
-    for copy in join_copies:
-        copy.start()
 
     @pl.when(jnp.logical_not(has_left))
     def _():
@@ -267,6 +254,19 @@
         for p in range(3):
             index = lax.broadcasted_iota(jnp.int32, (rows, rows), 0) + p * rows
             one_hot[p * rows : (p + 1) * rows, lanes] = jnp.where(line == index, 1.0, 0.0).astype(BF16)
+    pl.semaphore_wait(
+        barrier,
+        has_left.astype(jnp.int32) + has_right.astype(jnp.int32)
+        + (n_branch - 1 + near_group - 1 + far_group - 1),
+    )
+
+    loads[0].wait()
+    start(halo(0))
+    loads[3].wait()
+    join_copies = across(join, join_got, 0)
+    for copy in join_copies:
+        copy.start()
+
     for load in loads[4:]:
         load.wait()
     retained = foot[...].astype(F32)
@@ -393,9 +393,13 @@
         def _():
             sum_near(layer + 1)
 
+        @pl.when(step >= 2)
+        def _():
+            sum_far(layer + 2)
+
         @pl.when(step >= 3)
         def _():
-            sum_far(layer + 3)
+            finish(layer + 3)
 
         grad[...] = take_back(layer, inner)
 
@@ -403,23 +407,17 @@
     act = (masked * slope[0]).astype(BF16)
     weigh(0, act)
     inner = masked + spread(0, act)
-    if depth > 1:
-        sum_near(1)
-    for k in (3, 2):
-        if k < depth:
-            sum_far(k)
+    late = [k for k in (1, 2, 3) if k < depth]
+    for k, stage in zip(late, (sum_near, sum_far, finish)):
+        stage(k)
     sum_near(0)
-    for k in (5, 4):
-        if k < depth:
-            finish(k)
     if depth > 1:
         sum_far(1)
+    if depth > 2:
+        finish(2)
     map_own[...] = take_back(0, inner).astype(BF16)
     map_copy = pltpu.make_async_copy(map_own, map_out, local_sem.at[0])
     map_copy.start()
-    for k in (3, 2):
-        if k < depth:
-            finish(k)
     sum_far(0)
     if depth > 1:
         finish(1)

time: 62.5 us -> 62.5 us (level)
  no operation moved by 1% of the time
where the time goes in v4:
time: 62.5 us; the launch traced here: 62.3 us
  Pallas kernels  61.7 us (99%)
  between operations  0.64 us (1%)
    pallas_call x1, Pallas kernels, per_device(): pl.pallas_call(functools.partial(kernel, n_sky, n_branch, near_group), ou...  59.4 us
    pallas_call x1, Pallas kernels, per_device(): pl.pallas_call(functools.partial(scale_kernel, normalizer), out_shape=(ja...  2.26 us

profile of v4, /device:TPU:0, one launch (start us, length us, event | category | flops | bytes accessed | tf_op | source)
XLA Modules:
  0.0 62.3 jit_solution(13934951149662572729)
XLA Ops:
  0.6 59.4 %unet_backward.1 = (bf16[64,256]{1,0:T(8,128)(2,1)}, bf16[6,9,64,64]{3,2,1,0:T(8,128)(2,1)}) custom-call(bf16[64,256]{1,0:T(8,128)(2,1)} %bitcast.6, s32[1,256]{1,0:T(1,128)} %foot_in.1, s32[9,256]{1,0:T(8,128)} %nb_in.1, bf16[6,9,64,64]{3,2,1,0:T(8,128)(2,1)} %bitcast.5, bf16[64,256]{1,0:T(8,128)(2,1)} %bitcast.7, bf16[9,128,256]{2,1,0:T(8,128)(2,1)} %dec_in.1, ...), custom_call_target="tpu_custom_call" | custom-call | tf_op jit(solution)/shard_map/unet_backward/pallas_call | solution.py:514
  60.1 2.3 %scale_sums.1 = (bf16[64,256]{1,0:T(8,128)(2,1)}, f32[6,9,64,64]{3,2,1,0:T(8,128)}) custom-call(bf16[64,256]{1,0:T(8,128)(2,1)} %get-tuple-element.6.map_in, bf16[6,9,64,64]{3,2,1,0:T(8,128)(2,1)} %get-tuple-element.7.sums_in), custom_call_target="tpu_custom_call" | custom-call | tf_op jit(solution)/shard_map/scale_sums/pallas_call | solution.py:529

commit v5 on v4

--- a/solution.py
+++ b/solution.py
@@ -283,7 +283,7 @@
         for k in range(taps):
             tap = enc[layer, k]
             enc_flat[layer, :, k * chans : (k + 1) * chans] = tap
-            enc_t[layer, :, k * chans : (k + 1) * chans] = jnp.transpose(tap)
+            enc_t[layer, k * chans : (k + 1) * chans, :] = jnp.transpose(tap)
 
         def decode(step):
             low, high = dec_cuts[step], dec_cuts[step + 1]
@@ -334,7 +334,8 @@
 
         @pl.when(layer < depth - 1)
         def _():
-            start(halo(layer + 1))
+            for side in (distant, close):
+                start_side(halo(layer + 1), side)
 
         slope[layer] = sig * (1.0 + pre * (1.0 - sig))
 
@@ -365,17 +366,14 @@
             copy.start()
 
     def spread(layer, act):
-        def placed(part):
-            spots = [
-                matmul(act, one_hot_t[part, k * rows : (k + 1) * rows, :]).astype(BF16)
-                for k in range(taps)
-            ]
-            return matmul(enc_t[layer], jnp.concatenate(spots, axis=0))
-
+        terms = matmul(enc_t[layer], act).astype(BF16)
+        terms = jnp.concatenate(
+            [terms[k * chans : (k + 1) * chans] for k in range(taps)], axis=1
+        )
         for side in (distant, close):
-            edge[side, layer] = placed(1 + side).astype(BF16)
+            edge[side, layer] = matmul(terms, one_hot_t[1 + side]).astype(BF16)
             start_side(back(layer), side)
-        return placed(0)
+        return matmul(terms, one_hot_t[0])
 
     def take_back(layer, inner):
         wait_recv(back(layer))
@@ -485,7 +483,7 @@
         vmem((128, rows), jnp.int32),
         vmem((rows, 128), jnp.int32),
         vmem((depth, chans, taps * chans), BF16),
-        vmem((depth, chans, taps * chans), BF16),
+        vmem((depth, taps * chans, chans), BF16),
         vmem((chans, rows), F32),
         vmem((2,) + layers, BF16),
         vmem((2,) + layers, BF16),

time: 62.5 us -> 62.9 us (level)
  no operation moved by 1% of the time
where the time goes in v5:
time: 62.9 us; the launch traced here: 62.7 us
  Pallas kernels  62.1 us (99%)
  between operations  0.64 us (1%)
    pallas_call x1, Pallas kernels, per_device(): pl.pallas_call(functools.partial(kernel, n_sky, n_branch, near_group), ou...  59.8 us
    pallas_call x1, Pallas kernels, per_device(): pl.pallas_call(functools.partial(scale_kernel, normalizer), out_shape=(ja...  2.26 us

profile of v5, /device:TPU:0, one launch (start us, length us, event | category | flops | bytes accessed | tf_op | source)
XLA Modules:
  0.0 62.7 jit_solution(12167400842106370520)
XLA Ops:
  0.6 59.8 %unet_backward.1 = (bf16[64,256]{1,0:T(8,128)(2,1)}, bf16[6,9,64,64]{3,2,1,0:T(8,128)(2,1)}) custom-call(bf16[64,256]{1,0:T(8,128)(2,1)} %bitcast.6, s32[1,256]{1,0:T(1,128)} %foot_in.1, s32[9,256]{1,0:T(8,128)} %nb_in.1, bf16[6,9,64,64]{3,2,1,0:T(8,128)(2,1)} %bitcast.5, bf16[64,256]{1,0:T(8,128)(2,1)} %bitcast.7, bf16[9,128,256]{2,1,0:T(8,128)(2,1)} %dec_in.1, ...), custom_call_target="tpu_custom_call" | custom-call | tf_op jit(solution)/shard_map/unet_backward/pallas_call | solution.py:512
  60.5 2.3 %scale_sums.1 = (bf16[64,256]{1,0:T(8,128)(2,1)}, f32[6,9,64,64]{3,2,1,0:T(8,128)}) custom-call(bf16[64,256]{1,0:T(8,128)(2,1)} %get-tuple-element.6.map_in, bf16[6,9,64,64]{3,2,1,0:T(8,128)(2,1)} %get-tuple-element.7.sums_in), custom_call_target="tpu_custom_call" | custom-call | tf_op jit(solution)/shard_map/scale_sums/pallas_call | solution.py:527
